TPU v7x, 32 devices: a whole 2x2x4 slice. The times are simulated.
32 devices in a mesh: expert: 8 (over y, x, core), narrow: 4 (over z).
Axes of the slice: x: 2, y: 2, z: 4, core: 2. Of those that a mesh axis runs over, the one named last changes fastest.
Arguments:
- feats: bfloat16 [32768, 512], P(('expert', 'narrow')), may hold values from -6 to 6
- cotangent: bfloat16 [32768, 512], P(('expert', 'narrow')), may hold values from -0.59765625 to 0.59765625
- routes: int32 [32768, 1], P(('expert', 'narrow')), may hold values from 0 to 7; in each aligned block of 1024 rows (0 to 1023, 1024 to 2047, ...) at most 256 rows name the same one
- image_ids: int32 [32768], P(('expert', 'narrow')), may hold values from 0 to 255, as said below
- codes: bfloat16 [256, 48], replicated, may hold values from -6 to 6
- params: bfloat16 [8, 2096, 512], P('expert', 'narrow'), may hold values from -0.375 to 0.375
Outputs:
- out_rows: bfloat16 [32768, 512], P(('expert', 'narrow'))
- feat_grad: bfloat16 [32768, 512], P(('expert', 'narrow'))
- param_grad: float32 [8, 2096, 512], P('expert', 'narrow')
- code_grad: float32 [256, 48], P(('expert', 'narrow'))
Inputs may be any that keep to these rules, and one draw needn't show every extreme that they name: `routes`: among the rows of one device no expert is named more than 256 times, and on some device some expert is named exactly 256 times. `image_ids`: the rows of the device with flat index f over expert+narrow (expert index slowest) name only images f * 8 to f * 8 + 2 * 8 - 1, taken modulo 256.
All inputs are finite; a program needn't handle non-finite values.
Results may differ from a plain program's by a relative error of at most 0.017.
Values may be sent and summed in bfloat16 or wider, within the bound.
A program may use at most 128 MiB of HBM per device.

v0:
```python
import jax
import jax.numpy as jnp
from jax import lax
from jax.sharding import PartitionSpec as P

LAYERS = 4
ROWS_DEV = 1024
IMG_DEV = 8


def shifted(block, axis, distance):
    devices = range(lax.axis_size(axis))
    route = [((i - distance) % len(devices), i) for i in devices]
    return lax.ppermute(block, axis, route)


def forward(weights, row_block, code_rows, depth_count):
    feature_width = row_block.shape[1]
    code_matrix = weights[depth_count * feature_width :]
    current = row_block
    inputs = []
    preacts = []
    for layer_no in range(depth_count):
        inputs.append(current)
        layer_weights = weights[layer_no * feature_width : (layer_no + 1) * feature_width]
        preact = jnp.dot(current, layer_weights, preferred_element_type=jnp.float32)
        if layer_no == 0:
            preact = preact + jnp.dot(code_rows, code_matrix, preferred_element_type=jnp.float32)
        preacts.append(preact)
        current = jax.nn.silu(preact).astype(jnp.bfloat16)
    inputs.append(code_rows)
    return (current, tuple(inputs), tuple(preacts))


def backward(weights, preacts, cotangent, depth_count):
    feature_width = cotangent.shape[1]
    code_matrix = weights[depth_count * feature_width :]
    upstream = cotangent.astype(jnp.float32)
    errors = []
    for layer_no in range(depth_count - 1, -1, -1):
        preact = preacts[layer_no]
        sigmoid_value = jax.nn.sigmoid(preact)
        error_rows = (upstream * sigmoid_value * (1.0 + preact * (1.0 - sigmoid_value))).astype(
            jnp.bfloat16
        )
        errors.insert(0, error_rows)
        layer_weights = weights[layer_no * feature_width : (layer_no + 1) * feature_width]
        upstream = jnp.dot(error_rows, layer_weights.T, preferred_element_type=jnp.float32)
    code_back = jnp.dot(errors[0], code_matrix.T, preferred_element_type=jnp.float32).astype(
        jnp.bfloat16
    )
    return (upstream.astype(jnp.bfloat16), code_back, tuple(errors))


def param_terms(inputs, errors):
    depth_count = len(errors)
    blocks = []
    for layer_no in range(depth_count):
        blocks.append(
            jnp.dot(inputs[layer_no].T, errors[layer_no], preferred_element_type=jnp.float32)
        )
    blocks.append(jnp.dot(inputs[depth_count].T, errors[0], preferred_element_type=jnp.float32))
    return jnp.concatenate(blocks, axis=0)


def flatten(values):
    return values.reshape(values.shape[0] * values.shape[1], values.shape[2])


def unflatten(values, leading):
    return values.reshape(leading, values.shape[0] // leading, values.shape[1])


def send_back(outcome, feat_back, code_back):
    return (
        lax.all_to_all(outcome, "expert", split_axis=0, concat_axis=0, tiled=True),
        lax.all_to_all(feat_back, "expert", split_axis=0, concat_axis=0, tiled=True),
        lax.all_to_all(code_back, "expert", split_axis=0, concat_axis=0, tiled=True),
    )


def body(feats, cotangent, routes, image_ids, codes, params):
    peer_count = lax.axis_size("expert")
    capacity = 2 * ROWS_DEV // peer_count
    full_params = lax.all_gather(params, "narrow", axis=1, tiled=True)[0]
    targets = routes[:, 0]
    onehot = (targets[:, None] == jnp.arange(peer_count, dtype=jnp.int32)[None, :]).astype(
        jnp.int32
    )
    slot_ids = jnp.sum(jnp.cumsum(onehot, axis=0) * onehot, axis=1) - 1
    positions = targets * capacity + slot_ids
    code_rows = codes[image_ids]

    def pack_slots(values):
        holder = jnp.zeros((peer_count * capacity, values.shape[1]), values.dtype)
        return holder.at[positions].set(values).reshape(peer_count, capacity, values.shape[1])

    def owner_pass(pieces):
        got_rows, got_codes, got_cot = pieces
        leading = got_rows.shape[0]
        outcome, inputs, preacts = forward(
            full_params, flatten(got_rows), flatten(got_codes), LAYERS
        )
        feat_back, code_back, errors = backward(full_params, preacts, flatten(got_cot), LAYERS)
        came_back = send_back(
            unflatten(outcome, leading),
            unflatten(feat_back, leading),
            unflatten(code_back, leading),
        )
        kept_inputs = tuple((unflatten(member, leading) for member in inputs))
        kept_errors = tuple((unflatten(member, leading) for member in errors))
        return tuple(came_back) + kept_inputs + kept_errors

    results = owner_pass(
        (
            lax.all_to_all(pack_slots(feats), "expert", split_axis=0, concat_axis=0, tiled=True),
            lax.all_to_all(
                pack_slots(code_rows), "expert", split_axis=0, concat_axis=0, tiled=True
            ),
            lax.all_to_all(
                pack_slots(cotangent), "expert", split_axis=0, concat_axis=0, tiled=True
            ),
        )
    )
    back_out, back_feat, back_code = (results[0], results[1], results[2])
    inputs = tuple((flatten(member) for member in results[3 : 4 + LAYERS]))
    errors = tuple((flatten(member) for member in results[4 + LAYERS :]))
    grad_terms = param_terms(inputs, errors)
    param_grad = lax.psum_scatter(
        grad_terms[None].astype(jnp.bfloat16), "narrow", scatter_dimension=1, tiled=True
    ).astype(jnp.float32)
    out_rows = flatten(back_out)[positions]
    feat_grad = flatten(back_feat)[positions]
    code_row_grad = flatten(back_code)[positions]
    first_image = lax.axis_index(("expert", "narrow")) * IMG_DEV
    offsets = (image_ids - first_image) % codes.shape[0]
    picker = (jnp.arange(2 * IMG_DEV, dtype=jnp.int32)[:, None] == offsets[None, :]).astype(
        jnp.bfloat16
    )
    window = jnp.dot(picker, code_row_grad, preferred_element_type=jnp.float32)
    code_grad = window[:IMG_DEV] + shifted(window[IMG_DEV:], ("expert", "narrow"), 1)
    return (out_rows, feat_grad, param_grad, code_grad)


def solution(mesh):
    in_specs = (
        P(("expert", "narrow"), None),
        P(("expert", "narrow"), None),
        P(("expert", "narrow"), None),
        P(("expert", "narrow")),
        P(),
        P("expert", "narrow", None),
    )
    out_specs = (
        P(("expert", "narrow"), None),
        P(("expert", "narrow"), None),
        P("expert", "narrow", None),
        P(("expert", "narrow"), None),
    )
    return jax.shard_map(body, mesh=mesh, in_specs=in_specs, out_specs=out_specs, check_vma=False)
```

profile of v0, /device:TPU:0, one launch (start us, length us, event | category | flops | bytes accessed | tf_op | source)
XLA Modules:
  0.0 282.9 jit_solution(1124210850600480562)
XLA Ops:
  7.2 2.9 %copy.33 = bf16[1,524,512]{2,0,1:T(2,128)(2,1)} copy(bf16[1,524,512]{2,1,0:T(8,128)(2,1)} %param.11) | data formatting | bytes 1073152 | tf_op args[5]
  16.5 6.4 %scatter_custom_fusion.1 = bf16[2048,48]{1,0:T(8,128)(2,1)S(1)} fusion(s32[1024]{0:T(1024)S(1)} %bitcast.120, bf16[256,48]{1,0:T(8,128)(2,1)S(1)} %copy.35, s32[1024]{0:T(1024)S(1)} %get-tuple-element.31, bf16[]{:T(256)} %constant.38.clone.1), kind=kCustom, calls=%fused_computation.48 | custom fusion | bytes 196610 | tf_op jit(solution)/shard_map/scatter | solution.py:96
  23.8 5.2 %all-to-all-start.1 = ((bf16[8,256,48]{1,2,0:T(8,128)(2,1)}), bf16[8,256,48]{1,2,0:T(8,128)(2,1)S(1)}, u32[]{:S(2)}, u32[]{:S(2)}) async-start(bf16[8,256,48]{1,2,0:T(8,128)(2,1)} %copy.37), calls=%async_computation.1 | async-start | bytes 393216 | tf_op jit(solution)/shard_map/all_to_all | solution.py:117
  29.0 7.2 %scatter_custom_fusion = bf16[2048,512]{1,0:T(8,128)(2,1)} fusion(s32[1024]{0:T(1024)S(1)} %bitcast.121, bf16[1024,512]{1,0:T(8,128)(2,1)} %param.6, bf16[]{:T(256)} %constant.38.clone.1), kind=kCustom, calls=%fused_computation.41 | custom fusion | bytes 2097664 | tf_op jit(solution)/shard_map/scatter | solution.py:96
  36.2 4.2 %all-to-all-start = ((bf16[8,256,512]{2,1,0:T(8,128)(2,1)}), bf16[8,256,512]{2,1,0:T(8,128)(2,1)S(1)}, u32[]{:S(2)}, u32[]{:S(2)}) async-start(bf16[8,256,512]{2,1,0:T(8,128)(2,1)} %bitcast.110), calls=%async_computation | async-start | bytes 4194304 | tf_op jit(solution)/shard_map/all_to_all | solution.py:116
  40.4 7.4 %scatter_custom_fusion.2 = bf16[2048,512]{1,0:T(8,128)(2,1)} fusion(s32[1024]{0:T(1024)S(1)} %bitcast.122, bf16[1024,512]{1,0:T(8,128)(2,1)} %param.7, bf16[]{:T(256)} %constant.38.clone.1), kind=kCustom, calls=%fused_computation.39 | custom fusion | bytes 2097664 | tf_op jit(solution)/shard_map/scatter | solution.py:96
  47.8 47.5 %all-gather.2.cloned.1.call-done = bf16[1,2096,512]{2,0,1:T(2,128)(2,1)} async-done(((bf16[1,524,512]{2,0,1:T(2,128)(2,1)}), bf16[1,2096,512]{2,0,1:T(2,128)(2,1)}) %all-gather.2.cloned.1.call-update) | async-done | bytes 2146320 | tf_op jit(solution)/shard_map/all_gather | solution.py:85
  95.3 6.8 %fusion.31 = (bf16[1,512,512]{2,0,1:T(2,128)(2,1)S(1)}, bf16[1,512,512]{2,0,1:T(2,128)(2,1)}, bf16[1,512,512]{2,0,1:T(2,128)(2,1)}, bf16[1,512,512]{2,0,1:T(2,128)(2,1)}) fusion(bf16[1,2096,512]{2,0,1:T(2,128)(2,1)} %all-gather.2.cloned.1.call-done), kind=kLoop, calls=%fused_computation.78 | loop fusion | bytes 4194304 | tf_op jit(solution)/shard_map/slice | solution.py:25
  102.2 4.4 %all-to-all-start.3 = ((bf16[8,256,512]{2,1,0:T(8,128)(2,1)}), bf16[8,256,512]{2,1,0:T(8,128)(2,1)}, u32[]{:S(2)}, u32[]{:S(2)}) async-start(bf16[8,256,512]{2,1,0:T(8,128)(2,1)} %bitcast.109), calls=%async_computation.3 | async-start | bytes 4194304 | tf_op jit(solution)/shard_map/all_to_all | solution.py:120
  113.5 3.3 %fusion.22 = f32[2048,512]{1,0:T(8,128)} fusion(bf16[1,512,512]{2,0,1:T(2,128)(2,1)S(1)} %copy-done.6, f32[2048,512]{1,0:T(8,128)S(1)} %fusion.21), kind=kOutput, calls=%fused_computation.53 | convolution fusion | flops 1078984704 | bytes 8912896 | tf_op jit(solution)/shard_map/dot_general | solution.py:26
  116.8 16.3 %all-to-all-done.3 = bf16[8,256,512]{2,1,0:T(8,128)(2,1)} async-done(((bf16[8,256,512]{2,1,0:T(8,128)(2,1)}), bf16[8,256,512]{2,1,0:T(8,128)(2,1)}, u32[]{:S(2)}, u32[]{:S(2)}) %all-to-all-start.3) | async-done | bytes 2097184 | tf_op jit(solution)/shard_map/all_to_all | solution.py:120
  133.2 7.8 %fusion.2 = (bf16[2048,512]{1,0:T(8,128)(2,1)S(1)}, bf16[2048,512]{1,0:T(8,128)(2,1)}) fusion(bf16[8,256,512]{2,1,0:T(8,128)(2,1)} %all-to-all-done.3, bf16[1,512,512]{2,0,1:T(2,128)(2,1)} %get-tuple-element.27, f32[2048,512]{1,0:T(8,128)} %fusion.22), kind=kOutput, calls=%fused_computation.9 | convolution fusion | flops 1091567616 | bytes 11010048 | tf_op jit(solution)/shard_map/dot_general | solution.py:26
  144.2 11.8 %multiply_convert_fusion.1 = bf16[2048,512]{1,0:T(8,128)(2,1)S(1)} fusion(f32[2048,512]{1,0:T(8,128)S(1)} %copy-done.13, bf16[2048,512]{1,0:T(8,128)(2,1)S(1)} %multiply_convert_fusion.2, bf16[1,512,512]{2,0,1:T(2,128)(2,1)S(1)} %copy-done.7), kind=kOutput, calls=%fused_computation.11 | convolution fusion | flops 1083179008 | bytes 8912896 | tf_op jit(solution)/shard_map/dot_general | solution.py:48
  162.2 3.4 %all-to-all-start.5 = ((bf16[8,256,48]{1,2,0:T(8,128)(2,1)}), bf16[8,256,48]{1,2,0:T(8,128)(2,1)S(1)}, u32[]{:S(2)}, u32[]{:S(2)}) async-start(bf16[8,256,48]{1,2,0:T(8,128)(2,1)} %bitcast.100), calls=%async_computation.5 | async-start | bytes 393216 | tf_op jit(solution)/shard_map/all_to_all | solution.py:78
  165.6 5.0 %fusion.6 = bf16[1,2096,512]{2,1,0:T(8,128)(2,1)} fusion(bf16[1,2096,512]{2,1,0:T(8,128)(2,1)} %fusion.4, bf16[2048,512]{1,0:T(8,128)(2,1)} %copy-done.17, f32[2048,512]{1,0:T(8,128)} %copy-done.2), kind=kOutput, calls=%fused_computation.31 | convolution fusion | flops 1079246848 | bytes 6815744 | tf_op jit(solution)/shard_map/dot_general | solution.py:60
  171.8 3.6 %all-to-all-start.2 = ((bf16[8,256,512]{2,1,0:T(8,128)(2,1)}), bf16[8,256,512]{2,1,0:T(8,128)(2,1)S(1)}, u32[]{:S(2)}, u32[]{:S(2)}) async-start(bf16[8,256,512]{2,1,0:T(8,128)(2,1)} %bitcast.112), calls=%async_computation.2 | async-start | bytes 4194304 | tf_op jit(solution)/shard_map/all_to_all | solution.py:76
  175.4 5.1 %fusion.8 = bf16[1,2096,512]{2,1,0:T(8,128)(2,1)} fusion(bf16[1,2096,512]{2,1,0:T(8,128)(2,1)} %fusion.6, bf16[2048,512]{1,0:T(8,128)(2,1)} %copy-done.16, f32[2048,512]{1,0:T(8,128)} %copy-done.12), kind=kOutput, calls=%fused_computation.33 | convolution fusion | flops 1079246848 | bytes 6815744 | tf_op jit(solution)/shard_map/dot_general | solution.py:60
  183.7 2.6 convolution_convert_fusion
  186.4 15.6 %all-to-all-done.2 = bf16[8,256,512]{2,1,0:T(8,128)(2,1)S(1)} async-done(((bf16[8,256,512]{2,1,0:T(8,128)(2,1)}), bf16[8,256,512]{2,1,0:T(8,128)(2,1)S(1)}, u32[]{:S(2)}, u32[]{:S(2)}) %all-to-all-start.2) | async-done | bytes 2097184 | tf_op jit(solution)/shard_map/all_to_all | solution.py:76
  201.9 4.4 %all-to-all-start.4 = ((bf16[8,256,512]{2,1,0:T(8,128)(2,1)}), bf16[8,256,512]{2,1,0:T(8,128)(2,1)}, u32[]{:S(2)}, u32[]{:S(2)}) async-start(bf16[8,256,512]{2,1,0:T(8,128)(2,1)} %bitcast.111), calls=%async_computation.4 | async-start | bytes 4194304 | tf_op jit(solution)/shard_map/all_to_all | solution.py:77
  206.3 42.5 %fusion = bf16[528,512]{1,0:T(8,128)(2,1)S(1)} fusion(bf16[1,2096,512]{2,1,0:T(8,128)(2,1)} %fusion.12), kind=kCustom, calls=%all-reduce-scatter | all-reduce-scatter fusion | flops 1081345 | bytes 2687488
  253.1 3.2 %gather_fusion.2 = bf16[1024,48]{1,0:T(8,128)(2,1)S(1)} fusion(bf16[2048,48]{1,0:T(8,128)(2,1)S(1)} %bitcast.108, s32[1024]{0:T(1024)S(1)} %broadcast_clamp_fusion), kind=kCustom, calls=%fused_computation.3 | custom fusion | bytes 200704 | tf_op jit(solution)/shard_map/gather | solution.py:134
  263.8 5.1 %gather_fusion = bf16[1024,512]{1,0:T(8,128)(2,1)} fusion(bf16[2048,512]{1,0:T(8,128)(2,1)S(1)} %bitcast.105, s32[1024]{0:T(1024)S(1)} %broadcast_clamp_fusion), kind=kCustom, calls=%fused_computation.1 | custom fusion | bytes 2101248 | tf_op jit(solution)/shard_map/gather | solution.py:132
  268.9 7.0 %gather_fusion.1 = bf16[1024,512]{1,0:T(8,128)(2,1)} fusion(bf16[2048,512]{1,0:T(8,128)(2,1)} %bitcast.18, s32[1024]{0:T(1024)S(1)} %broadcast_clamp_fusion), kind=kCustom, calls=%fused_computation.2 | custom fusion | bytes 2101248 | tf_op jit(solution)/shard_map/gather | solution.py:133
  (79 shorter events, 39.2 us)
Async XLA Ops:
  7.2 88.2 %all-gather.2.cloned.1.call-start = ((), (), s32[]{:S(2)}) async-start(), calls=%async_computation.6 | async-start | bytes 5365760 | tf_op jit(solution)/shard_map/all_gather | solution.py:85
  23.8 12.3 %all-to-all-start.1 = ((bf16[8,256,48]{1,2,0:T(8,128)(2,1)}), bf16[8,256,48]{1,2,0:T(8,128)(2,1)S(1)}, u32[]{:S(2)}, u32[]{:S(2)}) async-start(bf16[8,256,48]{1,2,0:T(8,128)(2,1)} %copy.37), calls=%async_computation.1 | async-start | bytes 393216 | tf_op jit(solution)/shard_map/all_to_all | solution.py:117
  36.2 66.0 %all-to-all-start = ((bf16[8,256,512]{2,1,0:T(8,128)(2,1)}), bf16[8,256,512]{2,1,0:T(8,128)(2,1)S(1)}, u32[]{:S(2)}, u32[]{:S(2)}) async-start(bf16[8,256,512]{2,1,0:T(8,128)(2,1)} %bitcast.110), calls=%async_computation | async-start | bytes 4194304 | tf_op jit(solution)/shard_map/all_to_all | solution.py:116
  102.2 31.0 %all-to-all-start.3 = ((bf16[8,256,512]{2,1,0:T(8,128)(2,1)}), bf16[8,256,512]{2,1,0:T(8,128)(2,1)}, u32[]{:S(2)}, u32[]{:S(2)}) async-start(bf16[8,256,512]{2,1,0:T(8,128)(2,1)} %bitcast.109), calls=%async_computation.3 | async-start | bytes 4194304 | tf_op jit(solution)/shard_map/all_to_all | solution.py:120
  110.1 3.5 %copy-start.6 = (bf16[1,512,512]{2,0,1:T(2,128)(2,1)S(1)}, bf16[1,512,512]{2,0,1:T(2,128)(2,1)}, u32[]{:S(2)}) copy-start(bf16[1,512,512]{2,0,1:T(2,128)(2,1)} %get-tuple-element.25) | copy-start | bytes 1572868
  133.2 7.8 %copy-start.8 = (bf16[1,512,512]{2,0,1:T(2,128)(2,1)S(1)}, bf16[1,512,512]{2,0,1:T(2,128)(2,1)}, u32[]{:S(2)}) copy-start(bf16[1,512,512]{2,0,1:T(2,128)(2,1)} %get-tuple-element.27) | copy-start | bytes 1572868
  133.2 7.8 %copy-start.10 = (f32[2048,512]{1,0:T(8,128)S(1)}, f32[2048,512]{1,0:T(8,128)}, u32[]{:S(2)}) copy-start(f32[2048,512]{1,0:T(8,128)} %fusion.22) | copy-start | bytes 12582916
  141.0 2.5 copy-start.14
  141.0 2.5 copy-start.7
  141.0 3.3 %copy-start.13 = (f32[2048,512]{1,0:T(8,128)S(1)}, f32[2048,512]{1,0:T(8,128)}, u32[]{:S(2)}) copy-start(f32[2048,512]{1,0:T(8,128)} %copy-done.12) | copy-start | bytes 12582916
  144.2 11.8 %copy-start.16 = (bf16[2048,512]{1,0:T(8,128)(2,1)}, bf16[2048,512]{1,0:T(8,128)(2,1)S(1)}, u32[]{:S(2)}) copy-start(bf16[2048,512]{1,0:T(8,128)(2,1)S(1)} %multiply_convert_fusion.2) | copy-start | bytes 6291460
  144.2 11.8 %copy-start.3 = (f32[2048,512]{1,0:T(8,128)S(1)}, f32[2048,512]{1,0:T(8,128)}, u32[]{:S(2)}) copy-start(f32[2048,512]{1,0:T(8,128)} %copy-done.2) | copy-start | bytes 12582916
  144.2 11.8 %copy-start.5 = (bf16[1,512,512]{2,0,1:T(2,128)(2,1)S(1)}, bf16[1,512,512]{2,0,1:T(2,128)(2,1)}, u32[]{:S(2)}) copy-start(bf16[1,512,512]{2,0,1:T(2,128)(2,1)} %get-tuple-element.26) | copy-start | bytes 1572868
  156.1 2.6 copy-start.17
  158.6 2.1 copy-start
  162.2 9.6 %all-to-all-start.5 = ((bf16[8,256,48]{1,2,0:T(8,128)(2,1)}), bf16[8,256,48]{1,2,0:T(8,128)(2,1)S(1)}, u32[]{:S(2)}, u32[]{:S(2)}) async-start(bf16[8,256,48]{1,2,0:T(8,128)(2,1)} %bitcast.100), calls=%async_computation.5 | async-start | bytes 393216 | tf_op jit(solution)/shard_map/all_to_all | solution.py:78
  171.8 30.2 %all-to-all-start.2 = ((bf16[8,256,512]{2,1,0:T(8,128)(2,1)}), bf16[8,256,512]{2,1,0:T(8,128)(2,1)S(1)}, u32[]{:S(2)}, u32[]{:S(2)}) async-start(bf16[8,256,512]{2,1,0:T(8,128)(2,1)} %bitcast.112), calls=%async_computation.2 | async-start | bytes 4194304 | tf_op jit(solution)/shard_map/all_to_all | solution.py:76
  175.4 5.2 %copy-start.11 = (f32[2048,512]{1,0:T(8,128)S(1)}, f32[2048,512]{1,0:T(8,128)}, u32[]{:S(2)}) copy-start(f32[2048,512]{1,0:T(8,128)} %fusion.22) | copy-start | bytes 12582916
  175.4 5.2 %copy-start.15 = (bf16[2048,512]{1,0:T(8,128)(2,1)S(1)}, bf16[2048,512]{1,0:T(8,128)(2,1)}, u32[]{:S(2)}) copy-start(bf16[2048,512]{1,0:T(8,128)(2,1)} %copy-done.14) | copy-start | bytes 6291460
  180.5 2.1 copy-start.1
  186.4 64.4 %copy-start.9 = (u32[32]{0:T(128)S(1)}, u32[32]{0:T(128)}, u32[]{:S(2)}) copy-start(u32[32]{0:T(128)} %constant.53) | copy-start | bytes 388
  201.9 66.9 %all-to-all-start.4 = ((bf16[8,256,512]{2,1,0:T(8,128)(2,1)}), bf16[8,256,512]{2,1,0:T(8,128)(2,1)}, u32[]{:S(2)}, u32[]{:S(2)}) async-start(bf16[8,256,512]{2,1,0:T(8,128)(2,1)} %bitcast.111), calls=%async_computation.4 | async-start | bytes 4194304 | tf_op jit(solution)/shard_map/all_to_all | solution.py:77
  248.8 3.4 %collective-permute-start.1 = (bf16[12,512]{1,0:T(8,128)(2,1)S(1)}, bf16[12,512]{1,0:T(8,128)(2,1)S(1)}, u32[]{:S(2)}, u32[]{:S(2)}) collective-permute-start(bf16[12,512]{1,0:T(8,128)(2,1)S(1)} %slice.77), channel_id=1, source_target_pairs={{0,1},{1,2},{2,3},{4,5},{5,6},{6,7},{8,9},{9,10},{10,11},{12,13},{... | collective-permute-start | bytes 36872
  256.5 6.7 %collective-permute-start = (f32[8,48]{1,0:T(8,128)S(1)}, f32[8,48]{1,0:T(8,128)S(1)}, u32[]{:S(2)}, u32[]{:S(2)}) collective-permute-start(f32[8,48]{1,0:T(8,128)S(1)} %slice.76), channel_id=1, source_target_pairs={{31,0},{0,1},{1,2},{2,3},{3,4},{4,5},{5,6},{6,7},{7,8},{8,9},{9,10... | collective-permute-start | bytes 4616 | tf_op jit(solution)/shard_map/ppermute | solution.py:14
  (3 other events, 5.2 us)
Sparse Core Ops, SparseCore 0:
  10.2 85.0 all-gather.1
where the time goes:
time: 288 us; the launch traced here: 283 us
  waiting for transfers between devices  82.9 us (29%)
  local copies, waits for them, and re-layouts  56.7 us (20%)
  matrix products  50.1 us (17%)
  blocking collectives  42.5 us (15%)
  starting transfers between devices  29.4 us (10%)
  between operations  15.2 us (5%)
  other arithmetic  6.04 us (2%)
    all_gather x1, waiting for transfers between devices, body(): full_params = lax.all_gather(params, 'narrow', axis=1, tiled=True)[0]  47.5 us
    unnamed x1, blocking collectives  42.5 us
    scatter x3, local copies, waits for them, and re-layouts, pack_slots(): holder.at[positions].set(values)  20.9 us
    dot_general x4, matrix products, backward(): jnp.dot(error_rows, layer_weights.T, preferred_element_type=jnp.float32)  19.4 us
    all_to_all x1, waiting for transfers between devices, body(): lax.all_to_all(pack_slots(cotangent), 'expert', split_axis=0, concat_axis...  16.3 us
    all_to_all x1, waiting for transfers between devices, send_back(): lax.all_to_all(outcome, 'expert', split_axis=0, concat_axis=0, tiled=True)  15.6 us
    dot_general x4, matrix products, param_terms(): jnp.dot(inputs[layer_no].T, errors[layer_no], preferred_element_type=jnp....  14.4 us
    dot_general x4, matrix products, forward(): preact = jnp.dot(current, layer_weights, preferred_element_type=jnp.float32)  13.7 us
  transfers between devices with their start and end apart: 9, of which 6 were waited for; matrix products, arithmetic and copies ran while one was open for 40% of the time, Pallas kernels for 0%

commit v1 on v0

v1 whole, which is shorter than its diff:
```python
import functools

import jax
import jax.numpy as jnp
from jax import lax
from jax.experimental import pallas as pl
from jax.experimental.pallas import tpu as pltpu
from jax.sharding import PartitionSpec as P

LAYERS = 4
IMG_DEV = 8
GROUP = 256
LANES = 128
F32 = jnp.float32
BF16 = jnp.bfloat16


def xor(a, b, extent):
    total, bit = 0, 1
    while bit < extent:
        x = lax.rem(lax.div(a, bit), 2)
        y = lax.rem(lax.div(b, bit), 2)
        total = total + bit * (x + y - 2 * x * y)
        bit *= 2
    return total


def mm(a, b):
    return jnp.dot(a, b, preferred_element_type=F32)


def mm_nt(a, b):
    return lax.dot_general(a, b, (((1,), (1,)), ((), ())), preferred_element_type=F32)


def mm_tn(a, b):
    return lax.dot_general(a, b, (((0,), (0,)), ((), ())), preferred_element_type=F32)


def kernel(
    E, N, IMAGES, feats, cot, tgt_row, tgt_col, ids_row, codes, params,
    out_rows, feat_grad, param_grad, code_grad,
    send_a, send_b, send_i, send_w, send_d,
    recv_a, recv_b, recv_i, recv_w, recv_d, recv_o, recv_f,
    shards, wide, weights, code_w, acts, slopes, code_rows, pick, unpick, oh_col,
    half, half_in, sems, zsems, nsems,
):
    rows, width = feats.shape
    prows = param_grad.shape[0]
    cap = 2 * rows // E
    per = GROUP // cap
    groups = 2 * rows // GROUP
    me = lax.axis_index("expert")
    z = lax.axis_index("narrow")
    flat = me * N + z
    following = lax.rem(flat + 1, E * N)
    preceding = lax.rem(flat + E * N - 1, E * N)

    def peer(k):
        return {"expert": xor(me, k, E)}

    def at_flat(f):
        return {"expert": lax.div(f, N), "narrow": lax.rem(f, N)}

    barrier = pltpu.get_barrier_semaphore()
    for k in range(1, E):
        pl.semaphore_signal(barrier, inc=1, device_id=peer(k))
    for j in range(1, N):
        pl.semaphore_signal(barrier, inc=1, device_id={"narrow": lax.rem(z + j, N)})
    pl.semaphore_signal(barrier, inc=1, device_id=at_flat(following))
    pl.semaphore_signal(barrier, inc=1, device_id=at_flat(preceding))
    pl.semaphore_wait(barrier, E - 1 + N - 1 + 2)

    def chunk(ref, k):
        return ref.at[pl.ds(pl.multiple_of(k * cap, cap), cap)]

    def exchange(which, src, dst, k):
        return pltpu.make_async_remote_copy(
            src_ref=src, dst_ref=dst, send_sem=sems.at[which, 0, k],
            recv_sem=sems.at[which, 1, k], device_id=peer(k))

    def copy_a(k):
        return exchange(0, chunk(send_a, k), chunk(recv_a, k), k)

    def copy_b(k):
        return exchange(1, chunk(send_b, k), chunk(recv_b, k), k)

    def copy_o(k):
        return exchange(2, chunk(send_a, k), chunk(recv_o, k), k)

    def copy_f(k):
        return exchange(3, chunk(send_b, k), chunk(recv_f, k), k)

    def copy_i(k):
        return exchange(4, send_i.at[lax.div(k, per)], recv_i.at[k], k)

    def copy_w(k):
        return exchange(5, send_w.at[k], recv_w.at[k], k)

    def each_peer(g, act):
        for i in range(per):
            k = g * per + i

            @pl.when(k != 0)
            def _():
                act(k)

    def line(way, shard):
        return pltpu.make_async_remote_copy(
            src_ref=shards.at[shard], dst_ref=shards.at[shard],
            send_sem=zsems.at[way, 0, shard], recv_sem=zsems.at[way, 1, shard],
            device_id={"narrow": z + 1 - 2 * way})

    def relay(step, begin):
        up, down = z - step, z + step

        @pl.when((up >= 0) & (z + 1 < N))
        def _():
            begin(line(0, up))

        @pl.when((down < N) & (z > 0))
        def _():
            begin(line(1, down))

    shards[z] = params[...]
    relay(0, lambda copy: copy.start())

    number = lax.broadcasted_iota(jnp.int32, (E, rows), 0)
    partner = jnp.bitwise_xor(tgt_row[...], me)
    named = jnp.where(jnp.broadcast_to(partner, (E, rows)) == number, 1.0, 0.0)
    upper = jnp.where(
        lax.broadcasted_iota(jnp.int32, (rows, rows), 0)
        <= lax.broadcasted_iota(jnp.int32, (rows, rows), 1), 1.0, 0.0).astype(BF16)
    count = mm(named.astype(BF16), upper)
    slot = jnp.sum(named * count, axis=0, keepdims=True) - 1.0
    place = (partner * cap).astype(F32) + slot
    offset = ids_row[...] - flat * IMG_DEV
    offset = jnp.where(offset < 0, offset + IMAGES, offset) + 1
    offset8 = jnp.broadcast_to(offset.astype(F32), (8, rows)).astype(BF16)

    def pack_feats(i, carry):
        g = groups - 1 - i
        span = pl.ds(pl.multiple_of(g * GROUP, GROUP), GROUP)
        wanted = (lax.broadcasted_iota(jnp.int32, (GROUP, rows), 0) + g * GROUP).astype(F32)
        chosen = jnp.where(jnp.broadcast_to(place, (GROUP, rows)) == wanted, 1.0, 0.0).astype(BF16)
        pick[span, :] = chosen
        send_a[span, :] = mm(chosen, feats[...]).astype(BF16)
        send_i[g] = mm_nt(offset8, chosen)
        each_peer(g, lambda k: (copy_a(k).start(), copy_i(k).start()))
        return carry

    lax.fori_loop(0, groups, pack_feats, 0)
    recv_a[:cap, :] = send_a[:cap, :]
    recv_i[0] = send_i[0]

    def pack_cot(i, carry):
        g = groups - 1 - i
        span = pl.ds(pl.multiple_of(g * GROUP, GROUP), GROUP)
        send_b[span, :] = mm(pick[span, :], cot[...]).astype(BF16)
        each_peer(g, lambda k: copy_b(k).start())
        return carry

    lax.fori_loop(0, groups, pack_cot, 0)
    recv_b[:cap, :] = send_b[:cap, :]

    lane = lax.broadcasted_iota(jnp.int32, (rows, LANES), 1)
    partner_col = jnp.bitwise_xor(tgt_col[...], me)
    oh_col[...] = jnp.where(
        jnp.broadcast_to(partner_col, (rows, LANES)) == lane, 1.0, 0.0).astype(BF16)

    def unpick_tile(i, carry):
        span = pl.ds(pl.multiple_of(i * GROUP, GROUP), GROUP)
        lower = jnp.where(
            lax.broadcasted_iota(jnp.int32, (GROUP, rows), 1)
            <= lax.broadcasted_iota(jnp.int32, (GROUP, rows), 0) + i * GROUP, 1.0, 0.0).astype(BF16)
        mine = oh_col[span, :].astype(F32)
        seen = mm(lower, oh_col[...])
        base = (lax.broadcasted_iota(jnp.int32, (GROUP, LANES), 1) * cap - 1).astype(F32)
        where = jnp.sum(mine * (seen + base), axis=1, keepdims=True)
        index = lax.broadcasted_iota(jnp.int32, (GROUP, 2 * rows), 1).astype(F32)
        unpick[span, :] = jnp.where(
            jnp.broadcast_to(where, (GROUP, 2 * rows)) == index, 1.0, 0.0).astype(BF16)
        return carry

    for step in range(1, N):
        if step == 1:
            lax.fori_loop(0, rows // GROUP, unpick_tile, 0)

        @pl.when(z - step >= 0)
        def _():
            line(0, z - step).wait_recv()

        @pl.when(z + step < N)
        def _():
            line(1, z + step).wait_recv()

        if step < N - 1:
            relay(step, lambda copy: copy.start())

    depth = LAYERS * width
    for n in range(N):
        wide[n * prows : (n + 1) * prows, :] = shards[n].astype(F32)[:prows]
    weights[...] = wide[:depth, :].astype(BF16)
    code_w[...] = jnp.zeros_like(code_w)
    code_w[: N * prows - depth, :] = wide[depth : N * prows, :].astype(BF16)

    def picked_images(g, i):
        held = recv_i[g * per + i][0:1, :]
        image = (lax.broadcasted_iota(jnp.int32, (16, GROUP), 0) + 1).astype(F32)
        hit = jnp.broadcast_to(held, (16, GROUP)) == image
        if per > 1:
            inside = lax.div(lax.broadcasted_iota(jnp.int32, (16, GROUP), 1), cap) == i
            hit = hit & inside
        return jnp.where(hit, 1.0, 0.0).astype(BF16)

    def onward(t, carry):
        g = groups - 1 - t
        span = pl.ds(pl.multiple_of(g * GROUP, GROUP), GROUP)
        each_peer(g, lambda k: (copy_a(k).wait_recv(), copy_i(k).wait_recv()))
        looked = jnp.zeros((GROUP, LANES), F32)
        for i in range(per):
            source = xor(me, g * per + i, E) * N + z
            first = pl.multiple_of(source * IMG_DEV, IMG_DEV)
            looked = looked + mm_tn(picked_images(g, i), codes[pl.ds(first, 16), :].astype(BF16))
        looked = looked.astype(BF16)
        code_rows[span, :] = looked
        current = recv_a[span, :]
        for l in range(LAYERS):
            pre = mm(current, weights[l * width : (l + 1) * width, :])
            if l == 0:
                pre = pre + mm(looked, code_w[...])
            s = 1.0 / (1.0 + jnp.exp(-pre))
            current = (pre * s).astype(BF16)
            slopes[l, span, :] = (s * (1.0 + pre * (1.0 - s))).astype(BF16)
            if l < LAYERS - 1:
                acts[l, span, :] = current
        each_peer(g, lambda k: copy_a(k).wait_send())
        send_a[span, :] = current
        each_peer(g, lambda k: copy_o(k).start())
        return carry

    lax.fori_loop(0, groups, onward, 0)
    recv_o[:cap, :] = send_a[:cap, :]

    wide[...] = jnp.zeros_like(wide)

    def back(t, carry):
        g = groups - 1 - t
        span = pl.ds(pl.multiple_of(g * GROUP, GROUP), GROUP)
        each_peer(g, lambda k: (copy_b(k).wait_recv(), copy_b(k).wait_send()))
        up = recv_b[span, :].astype(F32)
        for l in range(LAYERS - 1, -1, -1):
            err = (up * slopes[l, span, :].astype(F32)).astype(BF16)
            slopes[l, span, :] = err
            up = mm_nt(err, weights[l * width : (l + 1) * width, :])
        send_b[span, :] = up.astype(BF16)
        each_peer(g, lambda k: copy_f(k).start())
        code_back = mm_nt(err, code_w[...]).astype(BF16)
        for i in range(per):
            send_w[g * per + i] = mm(picked_images(g, i), code_back)
        each_peer(g, lambda k: copy_w(k).start())
        for l in range(LAYERS):
            values = recv_a[span, :] if l == 0 else acts[l - 1, span, :]
            wide[l * width : (l + 1) * width, :] += mm_tn(values, slopes[l, span, :])
        wide[depth:, :] += mm_tn(code_rows[span, :], err)
        return carry

    lax.fori_loop(0, groups, back, 0)
    recv_f[:cap, :] = send_b[:cap, :]
    recv_w[0] = send_w[0]

    padded = shards.shape[1]
    for n in range(N):
        send_d[n] = wide[n * prows : n * prows + padded, :].astype(BF16)

    def copy_d(j):
        dest = lax.rem(z + j, N)
        return pltpu.make_async_remote_copy(
            src_ref=send_d.at[dest], dst_ref=recv_d.at[j], send_sem=zsems.at[2, 0, j],
            recv_sem=zsems.at[2, 1, j], device_id={"narrow": dest})

    for j in range(1, N):
        copy_d(j).start()

    each = recv_w[0]
    for k in range(1, E):
        copy_w(k).wait_recv()
        each = each + recv_w[k]
    half[...] = each[IMG_DEV:]
    pass_on = pltpu.make_async_remote_copy(
        src_ref=half, dst_ref=half_in, send_sem=nsems.at[0], recv_sem=nsems.at[1],
        device_id=at_flat(following))
    pass_on.start()

    for copy, held, result in ((copy_o, recv_o, out_rows), (copy_f, recv_f, feat_grad)):
        for k in range(1, E):
            copy(k).wait_recv()

        def unpack(i, carry, held=held, result=result):
            span = pl.ds(pl.multiple_of(i * GROUP, GROUP), GROUP)
            result[span, :] = mm(unpick[span, :], held[...]).astype(BF16)
            return carry

        lax.fori_loop(0, rows // GROUP, unpack, 0)

    pass_on.wait()
    code_grad[...] = each[:IMG_DEV] + half_in[...]

    for j in range(1, N):
        copy_d(j).wait_recv()
    total = send_d[z].astype(F32)
    for j in range(1, N):
        total = total + recv_d[j].astype(F32)
    param_grad[...] = total[:prows]

    for step in range(N - 1):
        relay(step, lambda copy: copy.wait_send())
    for j in range(1, N):
        copy_d(j).wait_send()
    for k in range(1, E):
        for copy in (copy_o, copy_f, copy_i, copy_w):
            copy(k).wait_send()


def body(E, N, feats, cotangent, routes, image_ids, codes, params):
    rows, width = feats.shape
    prows = params.shape[1]
    padded = -(-prows // 16) * 16
    images, code = codes.shape
    deep = LAYERS * width + LANES
    around = jnp.concatenate([codes, codes[:IMG_DEV]], axis=0).astype(F32)
    around = jnp.pad(around, ((0, 0), (0, LANES - code)))
    shard = jnp.pad(params[0], ((0, padded - prows), (0, 0)))
    vm = pl.BlockSpec(memory_space=pltpu.VMEM)
    slots = 2 * rows
    buffer = pltpu.VMEM((slots, width), BF16)
    per = GROUP // (slots // E)
    groups = slots // GROUP
    out_rows, feat_grad, param_grad, code_grad = pl.pallas_call(
        functools.partial(kernel, E, N, images),
        out_shape=[
            jax.ShapeDtypeStruct((rows, width), BF16),
            jax.ShapeDtypeStruct((rows, width), BF16),
            jax.ShapeDtypeStruct((prows, width), F32),
            jax.ShapeDtypeStruct((IMG_DEV, LANES), F32),
        ],
        in_specs=[vm] * 7,
        out_specs=[vm] * 4,
        scratch_shapes=[
            buffer, buffer,
            pltpu.VMEM((groups, 8, GROUP), F32),
            pltpu.VMEM((E, 16, LANES), F32),
            pltpu.VMEM((N, padded, width), BF16),
            buffer, buffer,
            pltpu.VMEM((E, 8, GROUP), F32),
            pltpu.VMEM((E, 16, LANES), F32),
            pltpu.VMEM((N, padded, width), BF16),
            buffer, buffer,
            pltpu.VMEM((N, padded, width), BF16),
            pltpu.VMEM((deep, width), F32),
            pltpu.VMEM((LAYERS * width, width), BF16),
            pltpu.VMEM((LANES, width), BF16),
            pltpu.VMEM((LAYERS - 1, slots, width), BF16),
            pltpu.VMEM((LAYERS, slots, width), BF16),
            pltpu.VMEM((slots, LANES), BF16),
            pltpu.VMEM((slots, rows), BF16),
            pltpu.VMEM((rows, slots), BF16),
            pltpu.VMEM((rows, LANES), BF16),
            pltpu.VMEM((IMG_DEV, LANES), F32),
            pltpu.VMEM((IMG_DEV, LANES), F32),
            pltpu.SemaphoreType.DMA((6, 2, E)),
            pltpu.SemaphoreType.DMA((3, 2, N)),
            pltpu.SemaphoreType.DMA((2,)),
        ],
        compiler_params=pltpu.CompilerParams(
            collective_id=0, has_side_effects=True, vmem_limit_bytes=60 * 1024 * 1024),
    )(
        feats, cotangent, routes.reshape(1, rows), routes,
        image_ids.reshape(1, rows), around, shard,
    )
    return out_rows, feat_grad, param_grad[None], code_grad[:, :code]


def solution(mesh):
    E, N = mesh.shape["expert"], mesh.shape["narrow"]
    rows = P(("expert", "narrow"), None)
    held = P("expert", "narrow", None)
    return jax.shard_map(
        functools.partial(body, E, N), mesh=mesh,
        in_specs=(rows, rows, rows, P(("expert", "narrow")), P(), held),
        out_specs=(rows, rows, held, rows), check_vma=False)
```

time: 288 us -> 130 us (0.45); the launches traced: 283 us -> 130 us
  Pallas kernels: 0 us -> 118 us
  waiting for transfers between devices: 82.9 us -> 0 us
  matrix products: 50.1 us -> 0 us
  local copies, waits for them, and re-layouts: 56.7 us -> 10 us
  blocking collectives: 42.5 us -> 0 us
  starting transfers between devices: 29.4 us -> 0 us
  between operations: 15.2 us -> 0.67 us
  other arithmetic: 6.04 us -> 0.68 us
    pallas_call x0 -> x1, Pallas kernels: none -> 118 us  [body(): pl.pallas_call(functools.partial(kernel, E, N, images), out_shape=[jax.Sh...]
    dot_general x16 -> x0, matrix products: 50.1 us -> none  [the longest x4 19.4 us: backward(): jnp.dot(error_rows, layer_weights.T, preferred_element_type=jnp.float32)]
    all_gather x1 -> x0, waiting for transfers between devices: 47.5 us -> none  [body(): full_params = lax.all_gather(params, 'narrow', axis=1, tiled=True)[0]]
    unnamed x1 -> x0, blocking collectives: 42.5 us -> none
    all_to_all x6 -> x0, waiting for transfers between devices: 33.1 us -> none  [the longest x1 16.3 us: body(): lax.all_to_all(pack_slots(cotangent), 'expert', split_axis=0, concat_axis...]
    all_to_all x6 -> x0, starting transfers between devices: 25.1 us -> none  [the longest x1 5.17 us: body(): lax.all_to_all(pack_slots(code_rows), 'expert', split_axis=0, concat_axis...]
    scatter x3 -> x0, local copies, waits for them, and re-layouts: 20.9 us -> none  [pack_slots(): holder.at[positions].set(values)]
    gather x3 -> x0, local copies, waits for them, and re-layouts: 15.3 us -> none  [the longest x1 6.98 us: body(): feat_grad = flatten(back_feat)[positions]]
  transfers between devices with their start and end apart: 9 -> 0, of which waited for: 6 -> 0; matrix products, arithmetic and copies ran while one was open for 40% -> 0% of each run, Pallas kernels for 0% -> 0%
where the time goes in v1:
time: 130 us
  Pallas kernels  118 us (91%)
  local copies, waits for them, and re-layouts  10 us (8%)
    pallas_call x1, Pallas kernels, body(): pl.pallas_call(functools.partial(kernel, E, N, images), out_shape=[jax.Sh...  118 us
    unnamed x14, local copies, waits for them, and re-layouts  9.2 us

profile of v1, /device:TPU:0, one launch (start us, length us, event | category | flops | bytes accessed | tf_op | source)
XLA Modules:
  0.0 129.8 jit_solution(7888104812015949936)
XLA Ops:
  0.6 0.0 copy-start.2
  0.6 0.9 copy.11
  1.6 0.7 fusion.3.codes
  2.2 1.7 %copy.12.tgt_col = s32[1024,1]{1,0:T(8,128)} copy(s32[1024,1]{0,1:T(1,128)} %param.8) | data formatting | bytes 8192 | tf_op args[2]
  3.9 0.0 copy-done.2
  4.0 0.8 pad.12.params
  4.8 118.5 %shard_map.93 = (bf16[1024,512]{1,0:T(8,128)(2,1)}, bf16[1024,512]{1,0:T(8,128)(2,1)}, f32[524,512]{1,0:T(8,128)}, f32[8,128]{1,0:T(8,128)}) custom-call(bf16[1024,512]{1,0:T(8,128)(2,1)} %feats.1, bf16[1024,512]{1,0:T(8,128)(2,1)} %cot.1, s32[1,1024]{1,0:T(1,128)} %bitcast.7, s32[1024,1]{1,0:T(8,128)} %copy.12.tgt_col, s32[1,1024]{1,0:T(1,128)} %bitcast.8, ...), custom_call_target="tpu_custom_call" | custom-call | tf_op jit(solution)/shard_map/pallas_call | solution.py:339
  123.3 0.0 copy-start.1
  123.3 3.4 %copy.13 = f32[1,524,512]{2,0,1:T(1,128)} copy(f32[1,524,512]{2,1,0:T(8,128)} %bitcast.5) | data formatting | bytes 2146304
  126.7 0.0 copy-done.1
  126.7 0.0 copy-start
  126.7 1.0 copy.17
  127.6 0.6 copy-done
  128.3 0.0 copy-start.3
  128.3 1.0 copy.18
  129.3 0.0 copy-done.3
  129.3 0.6 copy.19
  (1 shorter events, 0.0 us)
Async XLA Ops:
  0.6 3.3 %copy-start.2 = (bf16[1,524,512]{2,1,0:T(8,128)(2,1)S(1)}, bf16[1,524,512]{2,1,0:T(8,128)(2,1)}, u32[]{:S(2)}) copy-start(bf16[1,524,512]{2,1,0:T(8,128)(2,1)} %param.11) | copy-start | bytes 1609732
  123.3 3.4 %copy-start.1 = (bf16[1024,512]{1,0:T(8,128)(2,1)S(1)}, bf16[1024,512]{1,0:T(8,128)(2,1)}, u32[]{:S(2)}) copy-start(bf16[1024,512]{1,0:T(8,128)(2,1)} %get-tuple-element.20) | copy-start | bytes 3145732
  126.7 1.6 %copy-start = (bf16[1024,512]{1,0:T(8,128)(2,1)S(1)}, bf16[1024,512]{1,0:T(8,128)(2,1)}, u32[]{:S(2)}) copy-start(bf16[1024,512]{1,0:T(8,128)(2,1)} %get-tuple-element.21) | copy-start | bytes 3145732
  128.3 1.0 copy-start.3

commit v2 on v1

v2 whole, which is shorter than its diff:
```python
import functools

import jax
import jax.numpy as jnp
from jax import lax
from jax.experimental import pallas as pl
from jax.experimental.pallas import tpu as pltpu
from jax.sharding import PartitionSpec as P

LAYERS = 4
IMG_DEV = 8
GROUP = 256
LANES = 128
F32 = jnp.float32
BF16 = jnp.bfloat16


def xor(a, b, extent):
    total, bit = 0, 1
    while bit < extent:
        x = lax.rem(lax.div(a, bit), 2)
        y = lax.rem(lax.div(b, bit), 2)
        total = total + bit * (x + y - 2 * x * y)
        bit *= 2
    return total


def mm(a, b):
    return jnp.dot(a, b, preferred_element_type=F32)


def mm_nt(a, b):
    return lax.dot_general(a, b, (((1,), (1,)), ((), ())), preferred_element_type=F32)


def mm_tn(a, b):
    return lax.dot_general(a, b, (((0,), (0,)), ((), ())), preferred_element_type=F32)


def kernel(
    E, N, IMAGES, feats, cot, tgt_row, ids_row, codes_t, params,
    out_rows, feat_grad, param_grad, code_grad,
    send_a, send_b, send_i, send_w, send_d,
    recv_a, recv_b, recv_i, recv_w, recv_d, recv_o, recv_f,
    shards, wide, weights, code_w, acts, slopes, code_rows, pick, place_col,
    ups, codes, send_c, recv_c, half, half_in, sems, zsems, nsems,
):
    rows, width = feats.shape
    prows = params.shape[1]
    cap = 2 * rows // E
    per = GROUP // cap
    groups = 2 * rows // GROUP
    padded = shards.shape[1]
    depth = LAYERS * width
    extra = N * prows - depth
    me = lax.axis_index("expert")
    z = lax.axis_index("narrow")
    flat = me * N + z
    following = lax.rem(flat + 1, E * N)
    preceding = lax.rem(flat + E * N - 1, E * N)

    def peer(k):
        return {"expert": xor(me, k, E)}

    def at_flat(f):
        return {"expert": lax.div(f, N), "narrow": lax.rem(f, N)}

    barrier = pltpu.get_barrier_semaphore()
    for k in range(1, E):
        pl.semaphore_signal(barrier, inc=1, device_id=peer(k))
    for j in range(1, N):
        pl.semaphore_signal(barrier, inc=1, device_id={"narrow": lax.rem(z + j, N)})
    pl.semaphore_signal(barrier, inc=1, device_id=at_flat(following))
    pl.semaphore_signal(barrier, inc=1, device_id=at_flat(preceding))

    def chunk(ref, k):
        return ref.at[pl.ds(pl.multiple_of(k * cap, cap), cap)]

    def exchange(which, src, dst, k):
        return pltpu.make_async_remote_copy(
            src_ref=src, dst_ref=dst, send_sem=sems.at[which, 0, k],
            recv_sem=sems.at[which, 1, k], device_id=peer(k))

    def copy_a(k):
        return exchange(0, chunk(send_a, k), chunk(recv_a, k), k)

    def copy_b(k):
        return exchange(1, chunk(send_b, k), chunk(recv_b, k), k)

    def copy_o(k):
        return exchange(2, chunk(send_a, k), chunk(recv_o, k), k)

    def copy_f(k):
        return exchange(3, chunk(send_b, k), chunk(recv_f, k), k)

    def copy_i(k):
        return exchange(4, send_i.at[lax.div(k, per)], recv_i.at[k], k)

    def copy_w(k):
        return exchange(5, send_w.at[k], recv_w.at[k], k)

    def each_peer(g, act):
        for i in range(per):
            k = g * per + i

            @pl.when(k != 0)
            def _():
                act(k)

    def line(way, shard):
        return pltpu.make_async_remote_copy(
            src_ref=shards.at[shard], dst_ref=shards.at[shard],
            send_sem=zsems.at[way, 0, shard], recv_sem=zsems.at[way, 1, shard],
            device_id={"narrow": z + 1 - 2 * way})

    def relay(step, begin):
        up, down = z - step, z + step

        @pl.when((up >= 0) & (z + 1 < N))
        def _():
            begin(line(0, up))

        @pl.when((down < N) & (z > 0))
        def _():
            begin(line(1, down))

    number = lax.broadcasted_iota(jnp.int32, (E, rows), 0)
    partner = jnp.bitwise_xor(tgt_row[...], me)
    named = jnp.where(jnp.broadcast_to(partner, (E, rows)) == number, 1.0, 0.0)
    upper = jnp.where(
        lax.broadcasted_iota(jnp.int32, (rows, rows), 0)
        <= lax.broadcasted_iota(jnp.int32, (rows, rows), 1), 1.0, 0.0).astype(BF16)
    count = mm(named.astype(BF16), upper)
    slot = jnp.sum(named * count, axis=0, keepdims=True) - 1.0
    place = (partner * cap).astype(F32) + slot
    offset = ids_row[...] - flat * IMG_DEV
    offset = jnp.where(offset < 0, offset + IMAGES, offset) + 1
    offset8 = jnp.broadcast_to(offset.astype(F32), (8, rows)).astype(BF16)

    tail = prows // 16 * 16
    shards[z, tail:, :] = jnp.zeros((padded - tail, width), BF16)
    shards[z, :prows, :] = params[0]

    pl.semaphore_wait(barrier, E - 1 + N - 1 + 2)
    relay(0, lambda copy: copy.start())

    def pack_feats(i, carry):
        g = groups - 1 - i
        span = pl.ds(pl.multiple_of(g * GROUP, GROUP), GROUP)
        wanted = (lax.broadcasted_iota(jnp.int32, (GROUP, rows), 0) + g * GROUP).astype(F32)
        chosen = jnp.where(jnp.broadcast_to(place, (GROUP, rows)) == wanted, 1.0, 0.0).astype(BF16)
        pick[span, :] = chosen
        send_a[span, :] = mm(chosen, feats[...]).astype(BF16)
        send_i[g] = mm_nt(offset8, chosen)
        each_peer(g, lambda k: (copy_a(k).start(), copy_i(k).start()))
        return carry

    lax.fori_loop(0, groups, pack_feats, 0)
    recv_a[:cap, :] = send_a[:cap, :]
    recv_i[0] = send_i[0]

    def pass_shards(step):
        @pl.when(z - step >= 0)
        def _():
            line(0, z - step).wait_recv()

        @pl.when(z + step < N)
        def _():
            line(1, z + step).wait_recv()

        if step < N - 1:
            relay(step, lambda copy: copy.start())

    pass_shards(1)

    def pack_cot(i, carry):
        g = groups - 1 - i
        span = pl.ds(pl.multiple_of(g * GROUP, GROUP), GROUP)
        send_b[span, :] = mm(pick[span, :], cot[...]).astype(BF16)
        each_peer(g, lambda k: copy_b(k).start())
        return carry

    lax.fori_loop(0, groups, pack_cot, 0)
    recv_b[:cap, :] = send_b[:cap, :]

    turned = jnp.transpose(codes_t[...].astype(F32))
    codes[...] = jnp.zeros_like(codes)
    codes[:IMAGES, : turned.shape[1]] = turned
    codes[IMAGES:, : turned.shape[1]] = turned[:IMG_DEV]

    place_col[...] = jnp.transpose(jnp.broadcast_to(place, (LANES, rows)))

    def unpick_tile(i, carry):
        span = pl.ds(pl.multiple_of(i * GROUP, GROUP), GROUP)
        where = place_col[span, :][:, 0:1]
        for h in range(2):
            index = (lax.broadcasted_iota(jnp.int32, (GROUP, rows), 1) + h * rows).astype(F32)
            pick[pl.ds(pl.multiple_of(h * rows + i * GROUP, GROUP), GROUP), :] = jnp.where(
                jnp.broadcast_to(where, (GROUP, rows)) == index, 1.0, 0.0).astype(BF16)
        return carry

    lax.fori_loop(0, rows // GROUP, unpick_tile, 0)
    for step in range(2, N):
        pass_shards(step)

    for n in range(N):
        wide[n * prows : (n + 1) * prows, :] = shards[n].astype(F32)[:prows]
    weights[...] = wide[:depth, :].astype(BF16)
    code_w[...] = jnp.zeros_like(code_w)
    code_w[:extra, :] = wide[depth : N * prows, :].astype(BF16)

    def picked_images(g, i):
        held = recv_i[g * per + i][0:1, :]
        image = (lax.broadcasted_iota(jnp.int32, (16, GROUP), 0) + 1).astype(F32)
        hit = jnp.broadcast_to(held, (16, GROUP)) == image
        if per > 1:
            inside = lax.div(lax.broadcasted_iota(jnp.int32, (16, GROUP), 1), cap) == i
            hit = hit & inside
        return jnp.where(hit, 1.0, 0.0).astype(BF16)

    def both(t):
        pair = [groups - 1 - 2 * t, groups - 2 - 2 * t]
        return [(g, pl.ds(pl.multiple_of(g * GROUP, GROUP), GROUP)) for g in pair]

    def onward(t, carry):
        for g, span in both(t):
            each_peer(g, lambda k: (copy_a(k).wait_recv(), copy_i(k).wait_recv(), copy_a(k).wait_send()))
        current = []
        for g, span in both(t):
            looked = jnp.zeros((GROUP, LANES), F32)
            for i in range(per):
                source = xor(me, g * per + i, E) * N + z
                first = pl.multiple_of(source * IMG_DEV, IMG_DEV)
                looked = looked + mm_tn(picked_images(g, i), codes[pl.ds(first, 16), :].astype(BF16))
            code_rows[span, :] = looked.astype(BF16)
            current.append(recv_a[span, :])
        for l in range(LAYERS):
            pres = []
            for h, (g, span) in enumerate(both(t)):
                pre = mm(current[h], weights[l * width : (l + 1) * width, :])
                if l == 0:
                    pre = pre + mm(code_rows[span, :], code_w[...])
                pres.append(pre)
            for h, (g, span) in enumerate(both(t)):
                pre = pres[h]
                s = 1.0 / (1.0 + jnp.exp(-pre))
                z_l = (pre * s).astype(BF16)
                slopes[l, span, :] = (s * (1.0 + pre * (1.0 - s))).astype(BF16)
                if l < LAYERS - 1:
                    acts[l, span, :] = z_l
                else:
                    send_a[span, :] = z_l
                current[h] = z_l
        for g, span in both(t):
            each_peer(g, lambda k: copy_o(k).start())
        return carry

    lax.fori_loop(0, groups // 2, onward, 0)
    recv_o[:cap, :] = send_a[:cap, :]

    wide[...] = jnp.zeros_like(wide)

    def copy_d(dest, source):
        return pltpu.make_async_remote_copy(
            src_ref=send_d.at[dest], dst_ref=recv_d.at[source], send_sem=zsems.at[2, 0, dest],
            recv_sem=zsems.at[2, 1, source], device_id={"narrow": dest})

    def copy_c(source):
        return pltpu.make_async_remote_copy(
            src_ref=send_c, dst_ref=recv_c.at[source], send_sem=zsems.at[3, 0, 0],
            recv_sem=zsems.at[3, 1, source], device_id={"narrow": N - 1})

    for l in range(LAYERS - 1, -1, -1):
        rows_l = slice(l * width, (l + 1) * width)

        def back(t, carry, l=l, rows_l=rows_l):
            if l == LAYERS - 1:
                for g, span in both(t):
                    each_peer(g, lambda k: (copy_b(k).wait_recv(), copy_b(k).wait_send()))
            for g, span in both(t):
                up = recv_b[span, :].astype(F32) if l == LAYERS - 1 else ups[span, :]
                err = (up * slopes[l, span, :].astype(F32)).astype(BF16)
                slopes[l, span, :] = err
                if l > 0:
                    ups[span, :] = mm_nt(err, weights[rows_l, :])
            whole = pl.ds(pl.multiple_of((groups - 2 - 2 * t) * GROUP, 2 * GROUP), 2 * GROUP)
            values = recv_a[whole, :] if l == 0 else acts[l - 1, whole, :]
            wide[rows_l, :] += mm_tn(values, slopes[l, whole, :])
            if l == 0:
                wide[depth:, :] += mm_tn(code_rows[whole, :], slopes[l, whole, :])
            return carry

        lax.fori_loop(0, groups // 2, back, 0)
        if l == 0:
            send_c[...] = wide[depth : depth + extra, :].astype(BF16)

            @pl.when(z != N - 1)
            def _():
                copy_c(z).start()

        for n in range(N - 1, -1, -1):
            if n * prows // width == l:
                send_d[n] = wide[n * prows : n * prows + padded, :].astype(BF16)
                if n == N - 1:
                    start = depth - n * prows
                    send_d[n, start:, :] = jnp.zeros((padded - start, width), BF16)

                @pl.when(z != n)
                def _(n=n):
                    copy_d(n, z).start()

    def last(t, carry):
        for g, span in both(t):
            err = slopes[0, span, :]
            send_b[span, :] = mm_nt(err, weights[:width, :]).astype(BF16)
            code_back = mm_nt(err, code_w[...]).astype(BF16)
            for i in range(per):
                send_w[g * per + i] = mm(picked_images(g, i), code_back)
        for g, span in both(t):
            each_peer(g, lambda k: (copy_f(k).start(), copy_w(k).start()))
        return carry

    lax.fori_loop(0, groups // 2, last, 0)
    recv_f[:cap, :] = send_b[:cap, :]
    recv_w[0] = send_w[0]

    each = recv_w[0]
    for k in range(1, E):
        copy_w(k).wait_recv()
        each = each + recv_w[k]
    half[...] = each[IMG_DEV:]
    pass_on = pltpu.make_async_remote_copy(
        src_ref=half, dst_ref=half_in, send_sem=nsems.at[0], recv_sem=nsems.at[1],
        device_id=at_flat(following))
    pass_on.start()

    for copy, held, result in ((copy_o, recv_o, out_rows), (copy_f, recv_f, feat_grad)):
        for k in range(E // 2, E):
            copy(k).wait_recv()

        def upper_half(i, carry, held=held):
            span = pl.ds(pl.multiple_of(i * GROUP, GROUP), GROUP)
            second = pl.ds(pl.multiple_of(rows + i * GROUP, GROUP), GROUP)
            ups[span, :] = mm(pick[second, :], held[rows:, :])
            return carry

        lax.fori_loop(0, rows // GROUP, upper_half, 0)
        for k in range(1, E // 2):
            copy(k).wait_recv()

        def lower_half(i, carry, held=held, result=result):
            span = pl.ds(pl.multiple_of(i * GROUP, GROUP), GROUP)
            result[span, :] = (ups[span, :] + mm(pick[span, :], held[:rows, :])).astype(BF16)
            return carry

        lax.fori_loop(0, rows // GROUP, lower_half, 0)

    pass_on.wait()
    code_grad[...] = each[:IMG_DEV] + half_in[...]

    for j in range(1, N):
        copy_d(0, lax.rem(z + j, N)).wait_recv()
    total = send_d[z].astype(F32)
    for j in range(1, N):
        total = total + recv_d[lax.rem(z + j, N)].astype(F32)
    blocks = width // LANES
    for c in range(blocks):
        param_grad[pl.ds(c, prows, blocks), :] = total[:prows, c * LANES : (c + 1) * LANES]

    @pl.when(z == N - 1)
    def _():
        terms = send_c[...].astype(F32)
        for source in range(N - 1):
            copy_c(source).wait_recv()
            terms = terms + recv_c[source].astype(F32)
        start = (prows - extra) * blocks
        for c in range(blocks):
            param_grad[pl.ds(start + c, extra, blocks), :] = terms[:, c * LANES : (c + 1) * LANES]

    for step in range(N - 1):
        relay(step, lambda copy: copy.wait_send())
    for n in range(N):
        @pl.when(z != n)
        def _(n=n):
            copy_d(n, z).wait_send()

    @pl.when(z != N - 1)
    def _():
        copy_c(z).wait_send()

    for k in range(1, E):
        for copy in (copy_o, copy_f, copy_i, copy_w):
            copy(k).wait_send()


def body(E, N, feats, cotangent, routes, image_ids, codes, params):
    rows, width = feats.shape
    prows = params.shape[1]
    padded = -(-prows // 16) * 16
    images, code = codes.shape
    deep = LAYERS * width + LANES
    extra = N * prows - LAYERS * width
    vm = pl.BlockSpec(memory_space=pltpu.VMEM)
    slots = 2 * rows
    buffer = pltpu.VMEM((slots, width), BF16)
    per = GROUP // (slots // E)
    groups = slots // GROUP
    out_rows, feat_grad, param_grad, code_grad = pl.pallas_call(
        functools.partial(kernel, E, N, images),
        out_shape=[
            jax.ShapeDtypeStruct((rows, width), BF16),
            jax.ShapeDtypeStruct((rows, width), BF16),
            jax.ShapeDtypeStruct((prows * width // LANES, LANES), F32),
            jax.ShapeDtypeStruct((IMG_DEV, LANES), F32),
        ],
        in_specs=[vm] * 6,
        out_specs=[vm] * 4,
        scratch_shapes=[
            buffer, buffer,
            pltpu.VMEM((groups, 8, GROUP), F32),
            pltpu.VMEM((E, 16, LANES), F32),
            pltpu.VMEM((N, padded, width), BF16),
            buffer, buffer,
            pltpu.VMEM((E, 8, GROUP), F32),
            pltpu.VMEM((E, 16, LANES), F32),
            pltpu.VMEM((N, padded, width), BF16),
            buffer, buffer,
            pltpu.VMEM((N, padded, width), BF16),
            pltpu.VMEM((deep, width), F32),
            pltpu.VMEM((LAYERS * width, width), BF16),
            pltpu.VMEM((LANES, width), BF16),
            pltpu.VMEM((LAYERS - 1, slots, width), BF16),
            pltpu.VMEM((LAYERS, slots, width), BF16),
            pltpu.VMEM((slots, LANES), BF16),
            pltpu.VMEM((slots, rows), BF16),
            pltpu.VMEM((rows, LANES), F32),
            pltpu.VMEM((slots, width), F32),
            pltpu.VMEM((images + IMG_DEV, LANES), F32),
            pltpu.VMEM((extra, width), BF16),
            pltpu.VMEM((N, extra, width), BF16),
            pltpu.VMEM((IMG_DEV, LANES), F32),
            pltpu.VMEM((IMG_DEV, LANES), F32),
            pltpu.SemaphoreType.DMA((6, 2, E)),
            pltpu.SemaphoreType.DMA((4, 2, N)),
            pltpu.SemaphoreType.DMA((2,)),
        ],
        compiler_params=pltpu.CompilerParams(
            collective_id=0, has_side_effects=True, vmem_limit_bytes=60 * 1024 * 1024),
    )(
        feats, cotangent, routes.reshape(1, rows),
        image_ids.reshape(1, rows), codes.T, params,
    )
    return out_rows, feat_grad, param_grad.reshape(1, prows, width), code_grad[:, :code]


def solution(mesh):
    E, N = mesh.shape["expert"], mesh.shape["narrow"]
    rows = P(("expert", "narrow"), None)
    held = P("expert", "narrow", None)
    return jax.shard_map(
        functools.partial(body, E, N), mesh=mesh,
        in_specs=(rows, rows, rows, P(("expert", "narrow")), P(), held),
        out_specs=(rows, rows, held, rows), check_vma=False)
```

time: 130 us -> 124 us (0.954)
  local copies, waits for them, and re-layouts: 10 us -> 5.54 us
    unnamed x14 -> x10, local copies, waits for them, and re-layouts: 9.2 us -> 5.54 us
where the time goes in v2:
time: 124 us
  Pallas kernels  118 us (95%)
  local copies, waits for them, and re-layouts  5.54 us (4%)
    pallas_call x1, Pallas kernels, body(): pl.pallas_call(functools.partial(kernel, E, N, images), out_shape=[jax.Sh...  118 us
    unnamed x10, local copies, waits for them, and re-layouts  5.54 us

profile of v2, /device:TPU:0, one launch (start us, length us, event | category | flops | bytes accessed | tf_op | source)
XLA Modules:
  0.0 123.9 jit_solution(6232937076117863374)
XLA Ops:
  0.6 117.7 %shard_map.93 = (bf16[1024,512]{1,0:T(8,128)(2,1)}, bf16[1024,512]{1,0:T(8,128)(2,1)}, f32[2096,128]{1,0:T(8,128)}, f32[8,128]{1,0:T(8,128)}) custom-call(bf16[1024,512]{1,0:T(8,128)(2,1)} %feats.1, bf16[1024,512]{1,0:T(8,128)(2,1)} %cot.1, s32[1,1024]{1,0:T(1,128)} %bitcast.7, s32[1,1024]{1,0:T(1,128)} %bitcast.8, bf16[48,256]{1,0:T(8,128)(2,1)} %bitcast.6, ...), custom_call_target="tpu_custom_call" | custom-call | tf_op jit(solution)/shard_map/pallas_call | solution.py:408
  118.4 0.0 copy-start.1
  118.4 2.4 %copy.16 = bf16[1024,512]{1,0:T(8,128)(2,1)} copy(bf16[1024,512]{1,0:T(8,128)(2,1)} %get-tuple-element.24) | data formatting | bytes 2097152
  120.7 0.0 copy-done.1
  120.7 0.0 copy-start
  120.7 1.0 copy.17
  121.7 0.6 copy-done
  122.3 0.0 copy-start.2
  122.3 1.0 copy.18
  123.3 0.0 copy-done.2
  123.3 0.6 copy.19
Async XLA Ops:
  118.4 2.4 %copy-start.1 = (bf16[1024,512]{1,0:T(8,128)(2,1)S(1)}, bf16[1024,512]{1,0:T(8,128)(2,1)}, u32[]{:S(2)}) copy-start(bf16[1024,512]{1,0:T(8,128)(2,1)} %get-tuple-element.25) | copy-start | bytes 3145732
  120.7 1.6 %copy-start = (f32[2096,128]{1,0:T(8,128)S(1)}, f32[2096,128]{1,0:T(8,128)}, u32[]{:S(2)}) copy-start(f32[2096,128]{1,0:T(8,128)} %get-tuple-element.10) | copy-start | bytes 3219460
  122.3 1.0 copy-start.2

commit v3 on v2

--- a/solution.py
+++ b/solution.py
@@ -171,6 +171,12 @@
         if step < N - 1:
             relay(step, lambda copy: copy.start())
 
+    def widen(step):
+        for n in range(N):
+            @pl.when((z == n + step) | (z == n - step))
+            def _(n=n):
+                wide[n * prows : (n + 1) * prows, :] = shards[n].astype(F32)[:prows]
+
     pass_shards(1)
 
     def pack_cot(i, carry):
@@ -200,11 +206,12 @@
         return carry
 
     lax.fori_loop(0, rows // GROUP, unpick_tile, 0)
+    widen(0)
+    widen(1)
     for step in range(2, N):
         pass_shards(step)
-
-    for n in range(N):
-        wide[n * prows : (n + 1) * prows, :] = shards[n].astype(F32)[:prows]
+        widen(step)
+
     weights[...] = wide[:depth, :].astype(BF16)
     code_w[...] = jnp.zeros_like(code_w)
     code_w[:extra, :] = wide[depth : N * prows, :].astype(BF16)
@@ -218,44 +225,49 @@
             hit = hit & inside
         return jnp.where(hit, 1.0, 0.0).astype(BF16)
 
-    def both(t):
-        pair = [groups - 1 - 2 * t, groups - 2 - 2 * t]
-        return [(g, pl.ds(pl.multiple_of(g * GROUP, GROUP), GROUP)) for g in pair]
+    BLOCK = 2 * GROUP
+    steps = groups // 4
+
+    def four(t):
+        return [groups - 1 - 4 * t - i for i in range(4)]
+
+    def span_of(g, extent):
+        return pl.ds(pl.multiple_of(g * GROUP, extent), extent)
+
+    def halves(t):
+        return [span_of(groups - 2 - 4 * t, BLOCK), span_of(groups - 4 - 4 * t, BLOCK)]
 
     def onward(t, carry):
-        for g, span in both(t):
+        for g in four(t):
             each_peer(g, lambda k: (copy_a(k).wait_recv(), copy_i(k).wait_recv(), copy_a(k).wait_send()))
-        current = []
-        for g, span in both(t):
+        for g in four(t):
             looked = jnp.zeros((GROUP, LANES), F32)
             for i in range(per):
                 source = xor(me, g * per + i, E) * N + z
                 first = pl.multiple_of(source * IMG_DEV, IMG_DEV)
                 looked = looked + mm_tn(picked_images(g, i), codes[pl.ds(first, 16), :].astype(BF16))
-            code_rows[span, :] = looked.astype(BF16)
-            current.append(recv_a[span, :])
+            code_rows[span_of(g, GROUP), :] = looked.astype(BF16)
         for l in range(LAYERS):
             pres = []
-            for h, (g, span) in enumerate(both(t)):
-                pre = mm(current[h], weights[l * width : (l + 1) * width, :])
+            for span in halves(t):
+                current = recv_a[span, :] if l == 0 else acts[l - 1, span, :]
+                pre = mm(current, weights[l * width : (l + 1) * width, :])
                 if l == 0:
                     pre = pre + mm(code_rows[span, :], code_w[...])
                 pres.append(pre)
-            for h, (g, span) in enumerate(both(t)):
-                pre = pres[h]
-                s = 1.0 / (1.0 + jnp.exp(-pre))
-                z_l = (pre * s).astype(BF16)
-                slopes[l, span, :] = (s * (1.0 + pre * (1.0 - s))).astype(BF16)
+            for pre, span in zip(pres, halves(t)):
+                s = 0.5 + 0.5 * jnp.tanh(0.5 * pre)
+                z_l = pre * s
+                slopes[l, span, :] = (s + z_l * (1.0 - s)).astype(BF16)
                 if l < LAYERS - 1:
-                    acts[l, span, :] = z_l
+                    acts[l, span, :] = z_l.astype(BF16)
                 else:
-                    send_a[span, :] = z_l
-                current[h] = z_l
-        for g, span in both(t):
+                    send_a[span, :] = z_l.astype(BF16)
+        for g in four(t):
             each_peer(g, lambda k: copy_o(k).start())
         return carry
 
-    lax.fori_loop(0, groups // 2, onward, 0)
+    lax.fori_loop(0, steps, onward, 0)
     recv_o[:cap, :] = send_a[:cap, :]
 
     wide[...] = jnp.zeros_like(wide)
@@ -275,22 +287,22 @@
 
         def back(t, carry, l=l, rows_l=rows_l):
             if l == LAYERS - 1:
-                for g, span in both(t):
+                for g in four(t):
                     each_peer(g, lambda k: (copy_b(k).wait_recv(), copy_b(k).wait_send()))
-            for g, span in both(t):
+            for span in halves(t):
                 up = recv_b[span, :].astype(F32) if l == LAYERS - 1 else ups[span, :]
                 err = (up * slopes[l, span, :].astype(F32)).astype(BF16)
                 slopes[l, span, :] = err
                 if l > 0:
                     ups[span, :] = mm_nt(err, weights[rows_l, :])
-            whole = pl.ds(pl.multiple_of((groups - 2 - 2 * t) * GROUP, 2 * GROUP), 2 * GROUP)
+            whole = span_of(groups - 4 - 4 * t, 4 * GROUP)
             values = recv_a[whole, :] if l == 0 else acts[l - 1, whole, :]
             wide[rows_l, :] += mm_tn(values, slopes[l, whole, :])
             if l == 0:
                 wide[depth:, :] += mm_tn(code_rows[whole, :], slopes[l, whole, :])
             return carry
 
-        lax.fori_loop(0, groups // 2, back, 0)
+        lax.fori_loop(0, steps, back, 0)
         if l == 0:
             send_c[...] = wide[depth : depth + extra, :].astype(BF16)
 
@@ -310,13 +322,14 @@
                     copy_d(n, z).start()
 
     def last(t, carry):
-        for g, span in both(t):
+        for g in (groups - 1 - 2 * t, groups - 2 - 2 * t):
+            span = span_of(g, GROUP)
             err = slopes[0, span, :]
             send_b[span, :] = mm_nt(err, weights[:width, :]).astype(BF16)
             code_back = mm_nt(err, code_w[...]).astype(BF16)
             for i in range(per):
                 send_w[g * per + i] = mm(picked_images(g, i), code_back)
-        for g, span in both(t):
+        for g in (groups - 1 - 2 * t, groups - 2 - 2 * t):
             each_peer(g, lambda k: (copy_f(k).start(), copy_w(k).start()))
         return carry
 

time: 124 us -> 123 us (level)
  no operation moved by 1% of the time
where the time goes in v3:
time: 123 us
  Pallas kernels  117 us (95%)
  local copies, waits for them, and re-layouts  5.54 us (5%)
    pallas_call x1, Pallas kernels, body(): pl.pallas_call(functools.partial(kernel, E, N, images), out_shape=[jax.Sh...  117 us
    unnamed x10, local copies, waits for them, and re-layouts  5.54 us

profile of v3, /device:TPU:0, one launch (start us, length us, event | category | flops | bytes accessed | tf_op | source)
XLA Modules:
  0.0 122.9 jit_solution(15904615806515136993)
XLA Ops:
  0.6 116.8 %shard_map.93 = (bf16[1024,512]{1,0:T(8,128)(2,1)}, bf16[1024,512]{1,0:T(8,128)(2,1)}, f32[2096,128]{1,0:T(8,128)}, f32[8,128]{1,0:T(8,128)}) custom-call(bf16[1024,512]{1,0:T(8,128)(2,1)} %feats.1, bf16[1024,512]{1,0:T(8,128)(2,1)} %cot.1, s32[1,1024]{1,0:T(1,128)} %bitcast.7, s32[1,1024]{1,0:T(1,128)} %bitcast.8, bf16[48,256]{1,0:T(8,128)(2,1)} %bitcast.6, ...), custom_call_target="tpu_custom_call" | custom-call | tf_op jit(solution)/shard_map/pallas_call | solution.py:421
  117.4 0.0 copy-start.1
  117.4 2.4 %copy.16 = bf16[1024,512]{1,0:T(8,128)(2,1)} copy(bf16[1024,512]{1,0:T(8,128)(2,1)} %get-tuple-element.24) | data formatting | bytes 2097152
  119.8 0.0 copy-done.1
  119.8 0.0 copy-start
  119.8 1.0 copy.17
  120.7 0.6 copy-done
  121.4 0.0 copy-start.2
  121.4 1.0 copy.18
  122.3 0.0 copy-done.2
  122.4 0.6 copy.19
Async XLA Ops:
  117.4 2.4 %copy-start.1 = (bf16[1024,512]{1,0:T(8,128)(2,1)S(1)}, bf16[1024,512]{1,0:T(8,128)(2,1)}, u32[]{:S(2)}) copy-start(bf16[1024,512]{1,0:T(8,128)(2,1)} %get-tuple-element.25) | copy-start | bytes 3145732
  119.8 1.6 %copy-start = (f32[2096,128]{1,0:T(8,128)S(1)}, f32[2096,128]{1,0:T(8,128)}, u32[]{:S(2)}) copy-start(f32[2096,128]{1,0:T(8,128)} %get-tuple-element.10) | copy-start | bytes 3219460
  121.4 1.0 copy-start.2
